TPU v7x, 128 devices: a whole 4x4x4 slice. The times are simulated.
128 devices in a mesh: chan: 16 (over y, z_lo, core), tm: 8 (over x, z_hi).
Axes of the slice: x: 4, y: 4, z: 4 (z_hi: 2, z_lo: 2; z = z_hi * 2 + z_lo), core: 2. Of those that a mesh axis runs over, the one named last changes fastest.
Arguments:
- record: bfloat16 [256, 1024, 1024], P('chan', 'tm'), may hold values from -500 to 500
- flags: int32 [256], P('chan'), may hold values 0 or 1
Outputs:
- correlation: float32 [256, 256, 512], P('chan', 'tm')
Inputs may be any that keep to these rules, and one draw needn't show every extreme that they name: `flags`: 1 marks a usable channel, 0 a dead one.
All inputs are finite; a program needn't handle non-finite values. No bound on the sum of `flags` on one device may be relied on, other than what follows from the above.
Results may differ from a plain program's by a relative error of at most 0.0065.
Values may be sent and summed in bfloat16 or wider, within the bound.
No kernel may reach another device: no remote copies, remote signals or barrier semaphores. Data moves between devices by JAX's collectives and lax.ppermute only.
A program may use at most 256 MiB of HBM per device.

v0:
```python
import math

import jax
import jax.numpy as jnp
from jax import lax
from jax.sharding import PartitionSpec as P

F = 256
LAGS = 512
HALF = 64


def fourier_matrix(record_length):
    places = jnp.arange(record_length, dtype=jnp.int32)
    bins = jnp.arange(F, dtype=jnp.int32)
    phase = jnp.mod(places[:, None] * bins[None, :], record_length).astype(jnp.float32)
    angle = 2.0 * math.pi / record_length * phase
    return jnp.stack([jnp.cos(angle), -jnp.sin(angle)], axis=1).astype(jnp.bfloat16)


def lag_table(record_length, total_windows):
    bins = jnp.arange(F, dtype=jnp.int32)
    shifts = jnp.arange(LAGS, dtype=jnp.int32) - LAGS // 2
    phase = jnp.mod(bins[:, None] * shifts[None, :], record_length).astype(jnp.float32)
    angle = 2.0 * math.pi / record_length * phase
    factor = 1.0 / (F * total_windows)
    return jnp.stack([jnp.cos(angle) * factor, -jnp.sin(angle) * factor]).astype(jnp.bfloat16)


def whiten(record, flags):
    record_length = record.shape[2]
    places = jnp.arange(record_length, dtype=jnp.int32)
    band_mask = jnp.abs(places[:, None] - places[None, :]) <= HALF
    band = band_mask.astype(jnp.bfloat16)
    counts = jnp.sum(band_mask.astype(jnp.float32), axis=0)
    sums = jnp.einsum("cwl,lm->cwm", jnp.abs(record), band, preferred_element_type=jnp.float32)
    amplitude = sums / counts + 1e-05
    normalized = (record.astype(jnp.float32) / amplitude).astype(jnp.bfloat16)
    spectrum = jnp.einsum(
        "yjh,hqz->qzyj",
        normalized,
        fourier_matrix(record_length),
        preferred_element_type=jnp.float32,
    )
    power = spectrum[0] * spectrum[0] + spectrum[1] * spectrum[1]
    padded = jnp.pad(power, ((2, 2), (0, 0), (0, 0)))
    smoothing = (padded[0:-4] + padded[1:-3] + padded[2:-2] + padded[3:-1] + padded[4:]) / 5.0
    level = jnp.mean(power, axis=0, keepdims=True)
    scale = flags.astype(jnp.float32)[None, :, None] / jnp.sqrt(smoothing + 0.1 * level + 1e-06)
    return (spectrum * scale[None]).astype(jnp.bfloat16)


def cross_pair(local, remote):
    remote_swap = jnp.stack([-remote[1], remote[0]])
    real_part = jnp.einsum("sfcw,sfdw->fcd", local, remote, preferred_element_type=jnp.float32)
    imag_part = jnp.einsum("sfcw,sfdw->fcd", local, remote_swap, preferred_element_type=jnp.float32)
    return jnp.stack([real_part, imag_part]).astype(jnp.bfloat16)


def to_lags(blocks, table):
    return jnp.einsum("sfcd,sft->cdt", blocks, table, preferred_element_type=jnp.float32)


def per_device(record, flags):
    record_length = record.shape[2]
    total_windows = record.shape[1] * lax.axis_size("tm")
    white = whiten(record, flags)
    table = lag_table(record_length, total_windows)
    partial_value = to_lags(
        cross_pair(white, lax.all_gather(white, "chan", axis=2, tiled=True)), table
    )
    return lax.psum_scatter(partial_value, "tm", scatter_dimension=1, tiled=True)


def solution(mesh):
    return jax.shard_map(
        per_device,
        mesh=mesh,
        in_specs=(P("chan", "tm", None), P("chan")),
        out_specs=P("chan", "tm", None),
        check_vma=False,
    )
```

profile of v0, /device:TPU:1, one launch (start us, length us, event | category | flops | bytes accessed | tf_op | source)
XLA Modules:
  0.0 467.9 jit_solution(10647117311184485790)
XLA Ops:
  6.5 0.0 all-gather.2.cloned.1.call-start
  6.5 0.2 convert_reduce_fusion
  6.8 4.3 negate_convert_fusion
  11.1 0.7 convert_element_type.57
  11.7 12.7 %fusion.5 = f32[2,256,16,128]{3,1,2,0:T(8,128)} fusion(bf16[16,128,1024]{2,1,0:T(8,128)(2,1)} %param.2, f32[1024]{0:T(1024)S(1)} %convert_reduce_fusion, bf16[1024,1,256]{0,2,1:T(8,128)(2,1)S(1)} %get-tuple-element.11, bf16[1024,1,256]{0,2,1:T(8,128)(2,1)S(1)} %get-tuple-element.12), kind=kOutput, calls=%fused_computation.11 | convolution fusion | flops 6464471040 | bytes 9441280 | tf_op jit(solution)/shard_map/yjh,hqz->qzyj/dot_general | solution.py:39
  24.5 0.0 copy-start.1
  24.5 2.7 fusion.59
  27.2 1.2 rsqrt_multiply_fusion
  28.4 0.0 copy-done.1
  28.4 1.8 multiply_convert_fusion
  30.2 0.0 all-gather.2.cloned.1.call-update
  30.2 0.2 reduce-scatter.2.cloned.1.call-start
  30.5 2.3 multiply_convert_fusion.2
  32.7 171.9 %all-gather.2.cloned.1.call-done = bf16[2,256,256,128]{3,1,2,0:T(8,128)(2,1)} async-done(((bf16[2,256,16,128]{3,1,2,0:T(8,128)(2,1)}), bf16[2,256,256,128]{3,1,2,0:T(8,128)(2,1)}) %all-gather.2.cloned.1.call-update) | async-done | bytes 33554448 | tf_op jit(solution)/shard_map/all_gather | solution.py:70
  204.7 23.0 %slice_negate_fusion = (bf16[1,256,256,128]{3,1,2,0:T(8,128)(2,1)}, bf16[1,256,256,128]{3,1,2,0:T(8,128)(2,1)}) fusion(bf16[2,256,256,128]{3,1,2,0:T(8,128)(2,1)} %all-gather.2.cloned.1.call-done), kind=kLoop, calls=%fused_computation.5 | loop fusion | flops 8388608 | bytes 67108864 | tf_op jit(solution)/shard_map/neg | solution.py:54
  227.7 0.0 copy-start
  227.7 22.8 %pad_maximum_fusion = bf16[2,256,256,128]{3,1,2,0:T(8,128)(2,1)} fusion(bf16[1,256,256,128]{3,1,2,0:T(8,128)(2,1)} %get-tuple-element.6, bf16[1,256,256,128]{3,1,2,0:T(8,128)(2,1)} %get-tuple-element.5), kind=kLoop, calls=%fused_computation | loop fusion | flops 16777216 | bytes 67108864 | tf_op jit(solution)/shard_map/stack | solution.py:54
  250.5 0.0 copy-done
  250.5 43.0 %fusion.38 = bf16[1,256,16,256]{3,2,1,0:T(8,128)(2,1)} fusion(bf16[2,256,256,128]{3,1,2,0:T(8,128)(2,1)} %pad_maximum_fusion, bf16[2,256,16,128]{3,1,2,0:T(8,128)(2,1)S(1)} %copy-done), kind=kOutput, calls=%fused_computation.31 | convolution fusion | flops 537919488 | bytes 37748736 | tf_op jit(solution)/shard_map/sfcw,sfdw->fcd/dot_general | solution.py:56
  293.6 43.0 %fusion.33 = bf16[1,256,16,256]{3,2,1,0:T(8,128)(2,1)} fusion(bf16[2,256,256,128]{3,1,2,0:T(8,128)(2,1)} %all-gather.2.cloned.1.call-done, bf16[2,256,16,128]{3,1,2,0:T(8,128)(2,1)S(1)} %copy-done), kind=kOutput, calls=%fused_computation.30 | convolution fusion | flops 537919488 | bytes 37748736 | tf_op jit(solution)/shard_map/sfcw,sfdw->fcd/dot_general | solution.py:55
  336.6 2.6 pad_maximum_fusion.1
  339.2 6.9 %fusion.13 = f32[16,256,512]{2,1,0:T(8,128)} fusion(bf16[2,256,16,256]{3,2,1,0:T(8,128)(2,1)S(1)} %pad_maximum_fusion.1, bf16[1,256,512]{2,1,0:T(8,128)(2,1)S(1)} %get-tuple-element.10, bf16[1,256,512]{2,1,0:T(8,128)(2,1)S(1)} %get-tuple-element.9), kind=kOutput, calls=%fused_computation.21 | convolution fusion | flops 2147745792 | bytes 13107200 | tf_op jit(solution)/shard_map/sfcd,sft->cdt/dot_general | solution.py:61
  346.1 0.0 reduce-scatter.2.cloned.1.call-update
  346.2 114.9 %reduce-scatter.2.cloned.1.call-done = f32[16,32,512]{2,1,0:T(8,128)} async-done(((f32[16,256,512]{2,1,0:T(8,128)}), f32[16,32,512]{2,1,0:T(8,128)}) %reduce-scatter.2.cloned.1.call-update) | async-done | bytes 1048592 | tf_op jit(solution)/shard_map/reduce_scatter | solution.py:72
  (2 shorter events, 0.0 us)
Async XLA Ops:
  6.5 198.1 %all-gather.2.cloned.1.call-start = ((), (), s32[]{:S(2)}) async-start(), calls=%async_computation.1 | async-start | bytes 35651584 | tf_op jit(solution)/shard_map/all_gather | solution.py:70
  24.5 3.9 copy-start.1
  30.2 430.8 %reduce-scatter.2.cloned.1.call-start = ((), (), s32[]{:S(2)}) async-start(), calls=%async_computation.2 | async-start | bytes 9437184 | tf_op jit(solution)/shard_map/reduce_scatter | solution.py:72
  227.7 22.8 %copy-start = (bf16[2,256,16,128]{3,1,2,0:T(8,128)(2,1)S(1)}, bf16[2,256,16,128]{3,1,2,0:T(8,128)(2,1)}, u32[]{:S(2)}) copy-start(bf16[2,256,16,128]{3,1,2,0:T(8,128)(2,1)} %multiply_convert_fusion) | copy-start | bytes 6291460
Sparse Core Ops, SparseCore 0:
  30.3 174.2 all-gather.1
  346.3 114.7 reduce-scatter.1
where the time goes:
time: 468 us
  waiting for transfers between devices  287 us (61%)
  matrix products  106 us (23%)
  other arithmetic  61.6 us (13%)
  between operations  13.5 us (3%)
    all_gather x1, waiting for transfers between devices, per_device(): lax.all_gather(white, 'chan', axis=2, tiled=True)  172 us
    reduce_scatter x1, waiting for transfers between devices, per_device(): lax.psum_scatter(partial_value, 'tm', scatter_dimension=1, tiled=True)  115 us
    dot_general x1, matrix products, cross_pair(): jnp.einsum('sfcw,sfdw->fcd', local, remote_swap, preferred_element_type=j...  43 us
    dot_general x1, matrix products, cross_pair(): jnp.einsum('sfcw,sfdw->fcd', local, remote, preferred_element_type=jnp.fl...  43 us
    neg x1, other arithmetic, cross_pair(): remote_swap = jnp.stack([-remote[1], remote[0]])  23 us
    another operation x1, other arithmetic, cross_pair(): remote_swap = jnp.stack([-remote[1], remote[0]])  22.8 us
    dot_general x1, matrix products, whiten(): jnp.einsum('yjh,hqz->qzyj', normalized, fourier_matrix(record_length), pr...  12.7 us
  transfers between devices with their start and end apart: 2, of which 2 were waited for; matrix products, arithmetic and copies ran while one was open for 0% of the time, Pallas kernels for 0%

commit v1 on v0

v1 whole, which is shorter than its diff:
```python
import math

import jax
import jax.numpy as jnp
import ml_dtypes
import numpy as np
from jax import lax
from jax.experimental import pallas as pl
from jax.experimental.pallas import tpu as pltpu
from jax.sharding import PartitionSpec as P

L = 1024
F = 256
LAGS = 512
HALF = 64
CHANNELS = 256
WINDOWS = 1024
BOTH = ("chan", "tm")

CB = 4
NC = 16
NW = 128
ND = 32
N_CHAN = 16
N_TM = 8
N_DEV = 128
MIB = 1 << 20


def dft_rows():
    phase = np.outer(np.arange(F), np.arange(L)) % L
    angle = 2.0 * math.pi / L * phase
    parts = np.stack([np.cos(angle), -np.sin(angle)])
    parts = parts.reshape(2, 8, 32, L).transpose(0, 2, 1, 3)
    return parts.reshape(2 * F, L).astype(ml_dtypes.bfloat16)


def lag_rows():
    shifts = np.arange(LAGS) - LAGS // 2
    angle = 2.0 * math.pi / L * (np.outer(np.arange(F), shifts) % L)
    factor = 1.0 / (F * WINDOWS)
    parts = np.stack([np.cos(angle) * factor, -np.sin(angle) * factor])
    parts = parts.reshape(2, 128, 2, LAGS).transpose(2, 0, 1, 3)
    return parts.reshape(2 * F, LAGS).astype(ml_dtypes.bfloat16)


def band_block():
    rows = np.arange(512)[:, None] - 128
    return (np.abs(rows - np.arange(256)[None, :]) <= HALF).astype(ml_dtypes.bfloat16)


def inverse_counts():
    places = np.arange(L)
    counts = np.minimum(places + HALF, L - 1) - np.maximum(places - HALF, 0) + 1
    return (1.0 / counts).astype(np.float32).reshape(1, L)


def whiten_kernel(flags_ref, record_ref, band_ref, inverse_ref, table_ref, out_ref, wide):
    step = pl.program_id(0)
    rows = CB * NW
    x = record_ref[...].reshape(rows, L)
    magnitude = jnp.abs(x)
    pieces = []
    for j in range(4):
        low, high = max(256 * j - 128, 0), min(256 * j + 384, L)
        first = low - (256 * j - 128)
        sums = jnp.dot(
            magnitude[:, low:high],
            band_ref[first : first + high - low, :],
            preferred_element_type=jnp.float32,
        )
        cut = slice(256 * j, 256 * j + 256)
        amplitude = sums * inverse_ref[:, cut] + 1e-05
        pieces.append((x[:, cut].astype(jnp.float32) / amplitude).astype(jnp.bfloat16))
    normed = jnp.concatenate(pieces, axis=1)
    spectrum = lax.dot_general(
        table_ref[...], normed, (((1,), (1,)), ((), ())), preferred_element_type=jnp.float32
    )
    lanes = lax.broadcasted_iota(jnp.int32, (8, NW), 0)
    for c in range(CB):
        cut = slice(c * NW, (c + 1) * NW)
        real = [spectrum[8 * v : 8 * v + 8, cut] for v in range(32)]
        imag = [spectrum[F + 8 * v : F + 8 * v + 8, cut] for v in range(32)]
        power = [r * r + i * i for r, i in zip(real, imag)]
        before = [jnp.where(lanes == 0, 0.0, pltpu.roll(power[v], 1, 0)) for v in (30, 31)]
        after = [jnp.where(lanes == 7, 0.0, pltpu.roll(power[v], 7, 0)) for v in (0, 1)]
        padded = before + power + after
        total = power[0]
        for v in range(1, 32):
            total = total + power[v]
        floor = jnp.sum(total, axis=0, keepdims=True) * (0.1 / F) + 1e-06
        channel = step * CB + c
        flag = flags_ref[channel].astype(jnp.float32)
        for v in range(32):
            smooth = padded[v] + padded[v + 1] + padded[v + 2] + padded[v + 3] + padded[v + 4]
            scale = lax.rsqrt(smooth * 0.2 + floor) * flag
            for s, part in ((0, real), (1, imag)):
                place = ((v // 2) * 4 + s * 2 + v % 2) * NC + channel
                wide[pl.ds(place, 8, stride=64 * NC), :] = part[v] * scale

    @pl.when(step == pl.num_programs(0) - 1)
    def _():
        out_ref[...] = wide[...].astype(jnp.bfloat16)


def whiten(record, flags):
    rows = 2 * F * NC
    white = pl.pallas_call(
        whiten_kernel,
        grid=(NC // CB,),
        in_specs=[
            pl.BlockSpec(memory_space=pltpu.SMEM),
            pl.BlockSpec((CB, NW, L), lambda i: (i, 0, 0)),
            pl.BlockSpec((512, 256), lambda i: (0, 0)),
            pl.BlockSpec((1, L), lambda i: (0, 0)),
            pl.BlockSpec((2 * F, L), lambda i: (0, 0)),
        ],
        out_specs=pl.BlockSpec((rows, NW), lambda i: (0, 0)),
        out_shape=jax.ShapeDtypeStruct((rows, NW), jnp.bfloat16),
        scratch_shapes=[pltpu.VMEM((rows, NW), jnp.float32)],
        compiler_params=pltpu.CompilerParams(vmem_limit_bytes=40 * MIB),
        cost_estimate=pl.CostEstimate(flops=2 * 2048 * 1024 * 1024, bytes_accessed=8 * MIB, transcendentals=1 << 21),
    )(flags, record, band_block(), inverse_counts(), dft_rows())
    return white.reshape(N_DEV, 4, NC, NW)


def cross_kernel(white_ref, out_ref):
    spectra = []
    for g in range(2):
        parts = []
        for s in range(2):
            for j in range(N_TM):
                parts.append(white_ref[:, j, 2 * s + g].reshape(CHANNELS, NW))
        local = jnp.concatenate(parts, axis=1)
        turned = jnp.concatenate([-p for p in parts[N_TM:]] + parts[:N_TM], axis=1)
        remote = []
        for j in range(N_TM):
            cut = slice(ND * j, ND * j + ND)
            remote += [local[cut], turned[cut]]
        spectra.append(
            lax.dot_general(
                local, jnp.concatenate(remote, axis=0), (((1,), (1,)), ((), ())), preferred_element_type=jnp.float32
            )
        )
    for j in range(N_TM):
        cut = slice(2 * ND * j, 2 * ND * (j + 1))
        block = jnp.concatenate([spectra[0][:, cut], spectra[1][:, cut]], axis=1)
        out_ref[:, j] = block.astype(jnp.bfloat16).reshape(N_CHAN, NC, 4 * ND)


def cross(white):
    out = pl.pallas_call(
        cross_kernel,
        out_shape=jax.ShapeDtypeStruct((N_CHAN, N_TM, NC, 4 * ND), jnp.bfloat16),
        compiler_params=pltpu.CompilerParams(vmem_limit_bytes=40 * MIB),
        cost_estimate=pl.CostEstimate(flops=1 << 30, bytes_accessed=3 * MIB, transcendentals=0),
    )(white.reshape(N_CHAN, N_TM, 4, NC, NW))
    return out.reshape(N_DEV, NC, 4 * ND)


def lags_kernel(cross_ref, table_ref, out_ref, wide):
    wide[...] = cross_ref[...].astype(jnp.float32).reshape(N_DEV * NC, 4 * ND)
    rows = []
    for c in range(NC):
        bins = wide[pl.ds(c, N_DEV, stride=NC), :].T.astype(jnp.bfloat16)
        rows.append(jnp.concatenate([bins[ND * q : ND * q + ND] for q in range(4)], axis=1))
    out = jnp.dot(jnp.concatenate(rows, axis=0), table_ref[...], preferred_element_type=jnp.float32)
    out_ref[...] = out.reshape(NC, ND, LAGS)


def to_lags(spectra):
    return pl.pallas_call(
        lags_kernel,
        out_shape=jax.ShapeDtypeStruct((NC, ND, LAGS), jnp.float32),
        scratch_shapes=[pltpu.VMEM((N_DEV * NC, 4 * ND), jnp.float32)],
        compiler_params=pltpu.CompilerParams(vmem_limit_bytes=40 * MIB),
        cost_estimate=pl.CostEstimate(flops=1 << 28, bytes_accessed=2 * MIB, transcendentals=0),
    )(spectra, lag_rows())


def per_device(record, flags):
    white = lax.all_to_all(whiten(record, flags), BOTH, 0, 0, tiled=True)
    spectra = lax.all_to_all(cross(white), BOTH, 0, 0, tiled=True)
    return to_lags(spectra)


def solution(mesh):
    return jax.shard_map(
        per_device,
        mesh=mesh,
        in_specs=(P("chan", "tm", None), P("chan")),
        out_specs=P("chan", "tm", None),
        check_vma=False,
    )
```

time: 468 us -> 79.6 us (0.17)
  waiting for transfers between devices: 287 us -> 0 us
  matrix products: 106 us -> 0 us
  other arithmetic: 61.6 us -> 0 us
  blocking collectives: 0 us -> 60 us
  Pallas kernels: 0 us -> 13.6 us
  between operations: 13.5 us -> 0.02 us
  local copies, waits for them, and re-layouts: 0.01 us -> 5.71 us
    all_gather x1 -> x0, waiting for transfers between devices: 172 us -> none  [per_device(): lax.all_gather(white, 'chan', axis=2, tiled=True)]
    reduce_scatter x1 -> x0, waiting for transfers between devices: 115 us -> none  [per_device(): lax.psum_scatter(partial_value, 'tm', scatter_dimension=1, tiled=True)]
    dot_general x4 -> x0, matrix products: 106 us -> none  [the longest x1 43 us: cross_pair(): jnp.einsum('sfcw,sfdw->fcd', local, remote_swap, preferred_element_type=j...]
    all_to_all x0 -> x2, blocking collectives: none -> 60 us  [the longest x1 42 us: per_device(): white = lax.all_to_all(whiten(record, flags), BOTH, 0, 0, tiled=True)]
    another operation x4 -> x0, other arithmetic: 32 us -> none  [the longest x1 22.8 us: cross_pair(): remote_swap = jnp.stack([-remote[1], remote[0]])]
    neg x1 -> x0, other arithmetic: 23 us -> none  [cross_pair(): remote_swap = jnp.stack([-remote[1], remote[0]])]
    pallas_call x0 -> x3, Pallas kernels: none -> 13.6 us  [the longest x1 10.6 us: whiten(): pl.pallas_call(whiten_kernel, grid=(NC // CB,), in_specs=[pl.BlockSpec(me...]
    unnamed x4 -> x12, local copies, waits for them, and re-layouts: 0.01 us -> 5.71 us
  transfers between devices with their start and end apart: 2 -> 0, of which waited for: 2 -> 0; matrix products, arithmetic and copies ran while one was open for 0% -> 0% of each run, Pallas kernels for 0% -> 0%
where the time goes in v1:
time: 79.6 us; the launch traced here: 79.3 us
  blocking collectives  60 us (75%)
  Pallas kernels  13.6 us (17%)
  local copies, waits for them, and re-layouts  5.71 us (7%)
    all_to_all x1, blocking collectives, per_device(): white = lax.all_to_all(whiten(record, flags), BOTH, 0, 0, tiled=True)  42 us
    all_to_all x1, blocking collectives, per_device(): spectra = lax.all_to_all(cross(white), BOTH, 0, 0, tiled=True)  18 us
    pallas_call x1, Pallas kernels, whiten(): pl.pallas_call(whiten_kernel, grid=(NC // CB,), in_specs=[pl.BlockSpec(me...  10.6 us
    unnamed x12, local copies, waits for them, and re-layouts  5.71 us
    pallas_call x1, Pallas kernels, to_lags(): pl.pallas_call(lags_kernel, out_shape=jax.ShapeDtypeStruct((NC, ND, LAGS)...  1.69 us

profile of v1, /device:TPU:1, one launch (start us, length us, event | category | flops | bytes accessed | tf_op | source)
XLA Modules:
  0.0 79.3 jit_solution(6261680239636366111)
XLA Ops:
  0.0 0.0 copy-start.1
  0.0 2.2 %copy-done.1 = bf16[16,128,1024]{2,1,0:T(8,128)(2,1)S(1)} copy-done((bf16[16,128,1024]{2,1,0:T(8,128)(2,1)S(1)}, bf16[16,128,1024]{2,1,0:T(8,128)(2,1)}, u32[]{:S(2)}) %copy-start.1) | copy-done | bytes 4194328
  2.2 0.0 copy-start.2
  2.2 0.7 copy-done.2
  2.8 0.0 copy-start.3
  2.8 1.2 %copy-done.3 = bf16[512,1024]{1,0:T(8,128)(2,1)S(1)} copy-done((bf16[512,1024]{1,0:T(8,128)(2,1)S(1)}, bf16[512,1024]{1,0:T(8,128)(2,1)}, u32[]{:S(2)}) %copy-start.3) | copy-done | bytes 1048600
  4.1 0.0 copy-start.4
  4.1 0.9 %copy-done.4 = bf16[512,256]{1,0:T(8,128)(2,1)S(1)} copy-done((bf16[512,256]{1,0:T(8,128)(2,1)S(1)}, bf16[512,256]{1,0:T(8,128)(2,1)}, u32[]{:S(2)}) %copy-start.4) | copy-done | bytes 262168
  5.0 0.0 copy-start.5
  5.0 0.7 copy-done.5
  5.7 10.6 %shard_map.64 = bf16[8192,128]{1,0:T(8,128)(2,1)S(1)} custom-call(s32[16]{0:T(128)S(1)} %copy-done.2, bf16[16,128,1024]{2,1,0:T(8,128)(2,1)S(1)} %copy-done.1, bf16[512,256]{1,0:T(8,128)(2,1)S(1)} %copy-done.4, f32[1,1024]{1,0:T(1,128)S(1)} %copy-done.5, bf16[512,1024]{1,0:T(8,128)(2,1)S(1)} %copy-done.3), custom_call_target="tpu_custom_call" | custom-call | flops 4294967296 | bytes 8388608 | tf_op jit(solution)/shard_map/pallas_call | solution.py:108
  16.3 42.0 %all_to_all.10 = bf16[128,4,16,128]{3,2,1,0:T(8,128)(2,1)S(1)} all-to-all(bf16[128,4,16,128]{3,2,1,0:T(8,128)(2,1)S(1)} %bitcast.3), channel_id=1, replica_groups=mesh['chan'=16,'tm'=8] {'chan','tm'}, dimensions={0} | all-to-all | bytes 4194304 | tf_op jit(solution)/shard_map/all_to_all | solution.py:182
  58.2 0.0 copy-start
  58.2 1.4 %shard_map.65 = bf16[16,8,16,128]{3,2,1,0:T(8,128)(2,1)S(1)} custom-call(bf16[16,8,4,16,128]{4,3,2,1,0:T(8,128)(2,1)S(1)} %bitcast.4), custom_call_target="tpu_custom_call" | custom-call | flops 1073741824 | bytes 3145728 | tf_op jit(solution)/shard_map/pallas_call | solution.py:152
  59.6 18.0 %all_to_all.11.cross_ref = bf16[128,16,128]{2,1,0:T(8,128)(2,1)S(1)} all-to-all(bf16[128,16,128]{2,1,0:T(8,128)(2,1)S(1)} %bitcast.5), channel_id=1, replica_groups=mesh['chan'=16,'tm'=8] {'chan','tm'}, dimensions={0} | all-to-all | bytes 1048576 | tf_op jit(solution)/shard_map/all_to_all | solution.py:183
  77.6 0.0 copy-done
  77.6 1.7 %shard_map.66 = f32[16,32,512]{2,1,0:T(8,128)} custom-call(bf16[128,16,128]{2,1,0:T(8,128)(2,1)S(1)} %all_to_all.11.cross_ref, bf16[512,512]{1,0:T(8,128)(2,1)S(1)} %copy-done), custom_call_target="tpu_custom_call" | custom-call | flops 268435456 | bytes 2097152 | tf_op jit(solution)/shard_map/pallas_call | solution.py:172
Async XLA Ops:
  0.0 2.2 %copy-start.1 = (bf16[16,128,1024]{2,1,0:T(8,128)(2,1)S(1)}, bf16[16,128,1024]{2,1,0:T(8,128)(2,1)}, u32[]{:S(2)}) copy-start(bf16[16,128,1024]{2,1,0:T(8,128)(2,1)} %record_ref.1) | copy-start | bytes 12582916
  2.2 0.7 copy-start.2
  2.8 1.2 %copy-start.3 = (bf16[512,1024]{1,0:T(8,128)(2,1)S(1)}, bf16[512,1024]{1,0:T(8,128)(2,1)}, u32[]{:S(2)}) copy-start(bf16[512,1024]{1,0:T(8,128)(2,1)} %constant.10.clone.table_ref) | copy-start | bytes 3145732
  4.1 0.9 %copy-start.4 = (bf16[512,256]{1,0:T(8,128)(2,1)S(1)}, bf16[512,256]{1,0:T(8,128)(2,1)}, u32[]{:S(2)}) copy-start(bf16[512,256]{1,0:T(8,128)(2,1)} %constant.8.clone.band_ref) | copy-start | bytes 786436
  5.0 0.7 copy-start.5
  58.2 19.4 %copy-start = (bf16[512,512]{1,0:T(8,128)(2,1)S(1)}, bf16[512,512]{1,0:T(8,128)(2,1)}, u32[]{:S(2)}) copy-start(bf16[512,512]{1,0:T(8,128)(2,1)} %constant.11.clone.table_ref) | copy-start | bytes 1572868

commit v2 on v1

--- a/solution.py
+++ b/solution.py
@@ -17,7 +17,8 @@
 WINDOWS = 1024
 BOTH = ("chan", "tm")
 
-CB = 4
+SUB = 2
+PITCH = 17
 NC = 16
 NW = 128
 ND = 32
@@ -28,11 +29,11 @@
 
 
 def dft_rows():
-    phase = np.outer(np.arange(F), np.arange(L)) % L
+    phase = np.outer(np.arange(F), np.arange(L // 2)) % L
     angle = 2.0 * math.pi / L * phase
     parts = np.stack([np.cos(angle), -np.sin(angle)])
-    parts = parts.reshape(2, 8, 32, L).transpose(0, 2, 1, 3)
-    return parts.reshape(2 * F, L).astype(ml_dtypes.bfloat16)
+    parts = parts.reshape(2, 8, 16, 2, L // 2).transpose(3, 0, 2, 1, 4)
+    return parts.reshape(2, F, L // 2).astype(ml_dtypes.bfloat16)
 
 
 def lag_rows():
@@ -49,78 +50,108 @@
     return (np.abs(rows - np.arange(256)[None, :]) <= HALF).astype(ml_dtypes.bfloat16)
 
 
-def inverse_counts():
-    places = np.arange(L)
-    counts = np.minimum(places + HALF, L - 1) - np.maximum(places - HALF, 0) + 1
-    return (1.0 / counts).astype(np.float32).reshape(1, L)
-
-
-def whiten_kernel(flags_ref, record_ref, band_ref, inverse_ref, table_ref, out_ref, wide):
-    step = pl.program_id(0)
-    rows = CB * NW
-    x = record_ref[...].reshape(rows, L)
+def normalise(record, band):
+    x = record.reshape(SUB * NW, L)
     magnitude = jnp.abs(x)
-    pieces = []
+    quarters = []
     for j in range(4):
         low, high = max(256 * j - 128, 0), min(256 * j + 384, L)
         first = low - (256 * j - 128)
         sums = jnp.dot(
             magnitude[:, low:high],
-            band_ref[first : first + high - low, :],
+            band[first : first + high - low, :],
             preferred_element_type=jnp.float32,
         )
-        cut = slice(256 * j, 256 * j + 256)
-        amplitude = sums * inverse_ref[:, cut] + 1e-05
-        pieces.append((x[:, cut].astype(jnp.float32) / amplitude).astype(jnp.bfloat16))
-    normed = jnp.concatenate(pieces, axis=1)
-    spectrum = lax.dot_general(
-        table_ref[...], normed, (((1,), (1,)), ((), ())), preferred_element_type=jnp.float32
-    )
+        places = 256 * j + lax.broadcasted_iota(jnp.int32, (1, 256), 1)
+        counts = jnp.minimum(places + HALF, L - 1) - jnp.maximum(places - HALF, 0) + 1
+        amplitude = sums * (1.0 / counts.astype(jnp.float32)) + 1e-05
+        quarters.append(x[:, 256 * j : 256 * j + 256].astype(jnp.float32) / amplitude)
+    even = [(quarters[q] + quarters[q + 2]).astype(jnp.bfloat16) for q in range(2)]
+    odd = [(quarters[q] - quarters[q + 2]).astype(jnp.bfloat16) for q in range(2)]
+    return jnp.concatenate(even, axis=1), jnp.concatenate(odd, axis=1)
+
+
+def transform(table, halves):
+    return [
+        lax.dot_general(table[p], halves[p], (((1,), (1,)), ((), ())), preferred_element_type=jnp.float32)
+        for p in range(2)
+    ]
+
+
+def store_white(wide, spectra, flag, channel):
     lanes = lax.broadcasted_iota(jnp.int32, (8, NW), 0)
-    for c in range(CB):
-        cut = slice(c * NW, (c + 1) * NW)
-        real = [spectrum[8 * v : 8 * v + 8, cut] for v in range(32)]
-        imag = [spectrum[F + 8 * v : F + 8 * v + 8, cut] for v in range(32)]
-        power = [r * r + i * i for r, i in zip(real, imag)]
-        before = [jnp.where(lanes == 0, 0.0, pltpu.roll(power[v], 1, 0)) for v in (30, 31)]
-        after = [jnp.where(lanes == 7, 0.0, pltpu.roll(power[v], 7, 0)) for v in (0, 1)]
-        padded = before + power + after
-        total = power[0]
-        for v in range(1, 32):
-            total = total + power[v]
-        floor = jnp.sum(total, axis=0, keepdims=True) * (0.1 / F) + 1e-06
-        channel = step * CB + c
-        flag = flags_ref[channel].astype(jnp.float32)
-        for v in range(32):
-            smooth = padded[v] + padded[v + 1] + padded[v + 2] + padded[v + 3] + padded[v + 4]
-            scale = lax.rsqrt(smooth * 0.2 + floor) * flag
-            for s, part in ((0, real), (1, imag)):
-                place = ((v // 2) * 4 + s * 2 + v % 2) * NC + channel
-                wide[pl.ds(place, 8, stride=64 * NC), :] = part[v] * scale
-
-    @pl.when(step == pl.num_programs(0) - 1)
-    def _():
-        out_ref[...] = wide[...].astype(jnp.bfloat16)
+    place = [8 * (v // 2) for v in range(32)]
+    real = [spectra[v % 2][place[v] : place[v] + 8] for v in range(32)]
+    imag = [spectra[v % 2][F // 2 + place[v] : F // 2 + place[v] + 8] for v in range(32)]
+    power = [r * r + i * i for r, i in zip(real, imag)]
+    before = [jnp.where(lanes == 0, 0.0, pltpu.roll(power[v], 1, 0)) for v in (30, 31)]
+    after = [jnp.where(lanes == 7, 0.0, pltpu.roll(power[v], 7, 0)) for v in (0, 1)]
+    padded = before + power + after
+    total = power[0]
+    for v in range(1, 32):
+        total = total + power[v]
+    floor = jnp.sum(total, axis=0, keepdims=True) * (0.1 / F) + 1e-06
+    for v in range(32):
+        smooth = padded[v] + padded[v + 1] + padded[v + 2] + padded[v + 3] + padded[v + 4]
+        scale = lax.rsqrt(smooth * 0.2 + floor) * flag
+        for s, part in ((0, real), (1, imag)):
+            wide[pl.ds((2 * v + s) * 8 * PITCH + channel, 8, stride=PITCH), :] = part[v] * scale
+
+
+def whiten_kernel(flags_hbm, record_hbm, band_hbm, table_hbm, out_ref, record, band, table, wide, flags, sems):
+    count = NC // SUB
+    parts = [pl.ds(t * SUB, SUB) for t in range(count)]
+    copies = [pltpu.make_async_copy(record_hbm.at[p], record.at[p], sems.at[t]) for t, p in enumerate(parts)]
+    copies += [
+        pltpu.make_async_copy(band_hbm, band, sems.at[count]),
+        pltpu.make_async_copy(table_hbm, table, sems.at[count + 1]),
+        pltpu.make_async_copy(flags_hbm, flags, sems.at[count + 2]),
+    ]
+    for t in [0, count, 1, count + 1, count + 2, *range(2, count)]:
+        copies[t].start()
+    copies[count].wait()
+    halves, spectra = {}, {}
+    for t in range(count + 2):
+        if t < count:
+            copies[t].wait()
+            halves[t] = normalise(record[t * SUB : (t + 1) * SUB], band)
+        if t == 1:
+            copies[count + 1].wait()
+        if t == 2:
+            copies[count + 2].wait()
+        if 0 <= t - 1 < count:
+            spectra[t - 1] = transform(table, halves.pop(t - 1))
+        if 0 <= t - 2 < count:
+            even, odd = spectra.pop(t - 2)
+            for c in range(SUB):
+                cut = slice(c * NW, (c + 1) * NW)
+                channel = (t - 2) * SUB + c
+                store_white(wide, (even[:, cut], odd[:, cut]), flags[channel].astype(jnp.float32), channel)
+    for f in range(F):
+        for s in range(2):
+            place = ((2 * (f % 32) + s) * 8 + f // 32) * PITCH
+            row = ((f // 2) * 4 + 2 * s + f % 2) * NC
+            out_ref[row : row + NC, :] = wide[place : place + NC, :].astype(jnp.bfloat16)
 
 
 def whiten(record, flags):
     rows = 2 * F * NC
     white = pl.pallas_call(
         whiten_kernel,
-        grid=(NC // CB,),
-        in_specs=[
-            pl.BlockSpec(memory_space=pltpu.SMEM),
-            pl.BlockSpec((CB, NW, L), lambda i: (i, 0, 0)),
-            pl.BlockSpec((512, 256), lambda i: (0, 0)),
-            pl.BlockSpec((1, L), lambda i: (0, 0)),
-            pl.BlockSpec((2 * F, L), lambda i: (0, 0)),
+        in_specs=[pl.BlockSpec(memory_space=pltpu.HBM)] * 4,
+        out_specs=pl.BlockSpec(memory_space=pltpu.VMEM),
+        out_shape=jax.ShapeDtypeStruct((rows, NW), jnp.bfloat16),
+        scratch_shapes=[
+            pltpu.VMEM((NC, NW, L), jnp.bfloat16),
+            pltpu.VMEM((512, 256), jnp.bfloat16),
+            pltpu.VMEM((2, F, L // 2), jnp.bfloat16),
+            pltpu.VMEM((2 * F * PITCH, NW), jnp.float32),
+            pltpu.SMEM((NC,), jnp.int32),
+            pltpu.SemaphoreType.DMA((NC // SUB + 3,)),
         ],
-        out_specs=pl.BlockSpec((rows, NW), lambda i: (0, 0)),
-        out_shape=jax.ShapeDtypeStruct((rows, NW), jnp.bfloat16),
-        scratch_shapes=[pltpu.VMEM((rows, NW), jnp.float32)],
         compiler_params=pltpu.CompilerParams(vmem_limit_bytes=40 * MIB),
         cost_estimate=pl.CostEstimate(flops=2 * 2048 * 1024 * 1024, bytes_accessed=8 * MIB, transcendentals=1 << 21),
-    )(flags, record, band_block(), inverse_counts(), dft_rows())
+    )(*[pltpu.with_memory_space_constraint(jnp.asarray(a), pltpu.HBM) for a in (flags, record, band_block(), dft_rows())])
     return white.reshape(N_DEV, 4, NC, NW)
 
 

time: 79.6 us -> 70.7 us (0.89)
  local copies, waits for them, and re-layouts: 5.71 us -> 0.01 us
  Pallas kernels: 13.6 us -> 10.6 us
    unnamed x12 -> x2, local copies, waits for them, and re-layouts: 5.71 us -> 0.01 us
    pallas_call x1, Pallas kernels: 10.6 us -> 7.54 us  [whiten(): pl.pallas_call(whiten_kernel, in_specs=[pl.BlockSpec(memory_space=pltpu.H...]
where the time goes in v2:
time: 70.7 us; the launch traced here: 70.6 us
  blocking collectives  60 us (85%)
  Pallas kernels  10.6 us (15%)
    all_to_all x1, blocking collectives, per_device(): white = lax.all_to_all(whiten(record, flags), BOTH, 0, 0, tiled=True)  42 us
    all_to_all x1, blocking collectives, per_device(): spectra = lax.all_to_all(cross(white), BOTH, 0, 0, tiled=True)  18 us
    pallas_call x1, Pallas kernels, whiten(): pl.pallas_call(whiten_kernel, in_specs=[pl.BlockSpec(memory_space=pltpu.H...  7.54 us
    pallas_call x1, Pallas kernels, to_lags(): pl.pallas_call(lags_kernel, out_shape=jax.ShapeDtypeStruct((NC, ND, LAGS)...  1.69 us

profile of v2, /device:TPU:1, one launch (start us, length us, event | category | flops | bytes accessed | tf_op | source)
XLA Modules:
  0.0 70.6 jit_solution(3252506740957372183)
XLA Ops:
  0.0 7.5 %shard_map.55 = bf16[8192,128]{1,0:T(8,128)(2,1)S(1)} custom-call(s32[16]{0:T(128)} %flags_hbm.1, bf16[16,128,1024]{2,1,0:T(8,128)(2,1)} %record_hbm.1, bf16[512,256]{1,0:T(8,128)(2,1)} %constant.6.clone.band_hbm, bf16[2,256,512]{2,1,0:T(8,128)(2,1)} %constant.7.clone.table_hbm), custom_call_target="tpu_custom_call" | custom-call | flops 4294967296 | bytes 8388608 | tf_op jit(solution)/shard_map/pallas_call | solution.py:139
  7.6 42.0 %all_to_all.10 = bf16[128,4,16,128]{3,2,1,0:T(8,128)(2,1)S(1)} all-to-all(bf16[128,4,16,128]{3,2,1,0:T(8,128)(2,1)S(1)} %bitcast.3), channel_id=1, replica_groups=mesh['chan'=16,'tm'=8] {'chan','tm'}, dimensions={0} | all-to-all | bytes 4194304 | tf_op jit(solution)/shard_map/all_to_all | solution.py:213
  49.5 0.0 copy-start
  49.5 1.4 %shard_map.56 = bf16[16,8,16,128]{3,2,1,0:T(8,128)(2,1)S(1)} custom-call(bf16[16,8,4,16,128]{4,3,2,1,0:T(8,128)(2,1)S(1)} %bitcast.4), custom_call_target="tpu_custom_call" | custom-call | flops 1073741824 | bytes 3145728 | tf_op jit(solution)/shard_map/pallas_call | solution.py:183
  50.9 18.0 %all_to_all.11.cross_ref = bf16[128,16,128]{2,1,0:T(8,128)(2,1)S(1)} all-to-all(bf16[128,16,128]{2,1,0:T(8,128)(2,1)S(1)} %bitcast.5), channel_id=1, replica_groups=mesh['chan'=16,'tm'=8] {'chan','tm'}, dimensions={0} | all-to-all | bytes 1048576 | tf_op jit(solution)/shard_map/all_to_all | solution.py:214
  68.9 0.0 copy-done
  68.9 1.7 %shard_map.57 = f32[16,32,512]{2,1,0:T(8,128)} custom-call(bf16[128,16,128]{2,1,0:T(8,128)(2,1)S(1)} %all_to_all.11.cross_ref, bf16[512,512]{1,0:T(8,128)(2,1)S(1)} %copy-done), custom_call_target="tpu_custom_call" | custom-call | flops 268435456 | bytes 2097152 | tf_op jit(solution)/shard_map/pallas_call | solution.py:203
Async XLA Ops:
  49.5 19.4 %copy-start = (bf16[512,512]{1,0:T(8,128)(2,1)S(1)}, bf16[512,512]{1,0:T(8,128)(2,1)}, u32[]{:S(2)}) copy-start(bf16[512,512]{1,0:T(8,128)(2,1)} %constant.8.clone.table_ref) | copy-start | bytes 1572868

commit v3 on v2

--- a/solution.py
+++ b/solution.py
@@ -25,6 +25,7 @@
 N_CHAN = 16
 N_TM = 8
 N_DEV = 128
+N_OUT = 4
 MIB = 1 << 20
 
 
@@ -107,18 +108,18 @@
         pltpu.make_async_copy(table_hbm, table, sems.at[count + 1]),
         pltpu.make_async_copy(flags_hbm, flags, sems.at[count + 2]),
     ]
-    for t in [0, count, 1, count + 1, count + 2, *range(2, count)]:
+    for t in [0, 1, count, count + 1, count + 2, *range(2, count)]:
         copies[t].start()
-    copies[count].wait()
     halves, spectra = {}, {}
     for t in range(count + 2):
         if t < count:
-            copies[t].wait()
+            if t == 0:
+                for copy in copies[:2] + copies[count : count + 2]:
+                    copy.wait()
+            if t == 2:
+                for copy in copies[2:count] + copies[count + 2 :]:
+                    copy.wait()
             halves[t] = normalise(record[t * SUB : (t + 1) * SUB], band)
-        if t == 1:
-            copies[count + 1].wait()
-        if t == 2:
-            copies[count + 2].wait()
         if 0 <= t - 1 < count:
             spectra[t - 1] = transform(table, halves.pop(t - 1))
         if 0 <= t - 2 < count:
@@ -189,21 +190,34 @@
     return out.reshape(N_DEV, NC, 4 * ND)
 
 
-def lags_kernel(cross_ref, table_ref, out_ref, wide):
-    wide[...] = cross_ref[...].astype(jnp.float32).reshape(N_DEV * NC, 4 * ND)
-    rows = []
-    for c in range(NC):
-        bins = wide[pl.ds(c, N_DEV, stride=NC), :].T.astype(jnp.bfloat16)
-        rows.append(jnp.concatenate([bins[ND * q : ND * q + ND] for q in range(4)], axis=1))
-    out = jnp.dot(jnp.concatenate(rows, axis=0), table_ref[...], preferred_element_type=jnp.float32)
-    out_ref[...] = out.reshape(NC, ND, LAGS)
+def lags_kernel(cross_ref, table_ref, out_hbm, wide, lags, sems):
+    for k in range(N_DEV):
+        wide[k * PITCH : k * PITCH + NC, :] = cross_ref[k].astype(jnp.float32)
+    copies = []
+    for n in range(N_OUT):
+        rows = []
+        for c in range(n * NC // N_OUT, (n + 1) * NC // N_OUT):
+            bins = wide[pl.ds(c, N_DEV, stride=PITCH), :].T.astype(jnp.bfloat16)
+            rows.append(jnp.concatenate([bins[ND * q : ND * q + ND] for q in range(4)], axis=1))
+        out = jnp.dot(jnp.concatenate(rows, axis=0), table_ref[...], preferred_element_type=jnp.float32)
+        part = pl.ds(n * NC // N_OUT, NC // N_OUT)
+        lags[part] = out.reshape(NC // N_OUT, ND, LAGS)
+        copies.append(pltpu.make_async_copy(lags.at[part], out_hbm.at[part], sems.at[n]))
+        copies[n].start()
+    for copy in copies:
+        copy.wait()
 
 
 def to_lags(spectra):
     return pl.pallas_call(
         lags_kernel,
         out_shape=jax.ShapeDtypeStruct((NC, ND, LAGS), jnp.float32),
-        scratch_shapes=[pltpu.VMEM((N_DEV * NC, 4 * ND), jnp.float32)],
+        out_specs=pl.BlockSpec(memory_space=pltpu.HBM),
+        scratch_shapes=[
+            pltpu.VMEM((N_DEV * PITCH, 4 * ND), jnp.float32),
+            pltpu.VMEM((NC, ND, LAGS), jnp.float32),
+            pltpu.SemaphoreType.DMA((N_OUT,)),
+        ],
         compiler_params=pltpu.CompilerParams(vmem_limit_bytes=40 * MIB),
         cost_estimate=pl.CostEstimate(flops=1 << 28, bytes_accessed=2 * MIB, transcendentals=0),
     )(spectra, lag_rows())

time: 70.7 us -> 69.3 us (0.980)
  Pallas kernels: 10.6 us -> 9.12 us
    pallas_call x1, Pallas kernels: 7.54 us -> 6.41 us  [whiten(): pl.pallas_call(whiten_kernel, in_specs=[pl.BlockSpec(memory_space=pltpu.H...]
where the time goes in v3:
time: 69.3 us; the launch traced here: 69.1 us
  blocking collectives  60 us (87%)
  Pallas kernels  9.12 us (13%)
    all_to_all x1, blocking collectives, per_device(): white = lax.all_to_all(whiten(record, flags), BOTH, 0, 0, tiled=True)  42 us
    all_to_all x1, blocking collectives, per_device(): spectra = lax.all_to_all(cross(white), BOTH, 0, 0, tiled=True)  18 us
    pallas_call x1, Pallas kernels, whiten(): pl.pallas_call(whiten_kernel, in_specs=[pl.BlockSpec(memory_space=pltpu.H...  6.41 us

profile of v3, /device:TPU:1, one launch (start us, length us, event | category | flops | bytes accessed | tf_op | source)
XLA Modules:
  0.0 69.1 jit_solution(14696357649572803541)
XLA Ops:
  0.0 6.4 %shard_map.55 = bf16[8192,128]{1,0:T(8,128)(2,1)S(1)} custom-call(s32[16]{0:T(128)} %flags_hbm.1, bf16[16,128,1024]{2,1,0:T(8,128)(2,1)} %record_hbm.1, bf16[512,256]{1,0:T(8,128)(2,1)} %constant.6.clone.band_hbm, bf16[2,256,512]{2,1,0:T(8,128)(2,1)} %constant.7.clone.table_hbm), custom_call_target="tpu_custom_call" | custom-call | flops 4294967296 | bytes 8388608 | tf_op jit(solution)/shard_map/pallas_call | solution.py:140
  6.4 42.0 %all_to_all.10 = bf16[128,4,16,128]{3,2,1,0:T(8,128)(2,1)S(1)} all-to-all(bf16[128,4,16,128]{3,2,1,0:T(8,128)(2,1)S(1)} %bitcast.3), channel_id=1, replica_groups=mesh['chan'=16,'tm'=8] {'chan','tm'}, dimensions={0} | all-to-all | bytes 4194304 | tf_op jit(solution)/shard_map/all_to_all | solution.py:227
  48.4 0.0 copy-start
  48.4 1.4 %shard_map.56 = bf16[16,8,16,128]{3,2,1,0:T(8,128)(2,1)S(1)} custom-call(bf16[16,8,4,16,128]{4,3,2,1,0:T(8,128)(2,1)S(1)} %bitcast.4), custom_call_target="tpu_custom_call" | custom-call | flops 1073741824 | bytes 3145728 | tf_op jit(solution)/shard_map/pallas_call | solution.py:184
  49.8 18.0 %all_to_all.11.cross_ref = bf16[128,16,128]{2,1,0:T(8,128)(2,1)S(1)} all-to-all(bf16[128,16,128]{2,1,0:T(8,128)(2,1)S(1)} %bitcast.5), channel_id=1, replica_groups=mesh['chan'=16,'tm'=8] {'chan','tm'}, dimensions={0} | all-to-all | bytes 1048576 | tf_op jit(solution)/shard_map/all_to_all | solution.py:228
  67.8 0.0 copy-done
  67.8 1.4 %shard_map.57 = f32[16,32,512]{2,1,0:T(8,128)} custom-call(bf16[128,16,128]{2,1,0:T(8,128)(2,1)S(1)} %all_to_all.11.cross_ref, bf16[512,512]{1,0:T(8,128)(2,1)S(1)} %copy-done), custom_call_target="tpu_custom_call" | custom-call | flops 268435456 | bytes 2097152 | tf_op jit(solution)/shard_map/pallas_call | solution.py:212
Async XLA Ops:
  48.4 19.4 %copy-start = (bf16[512,512]{1,0:T(8,128)(2,1)S(1)}, bf16[512,512]{1,0:T(8,128)(2,1)}, u32[]{:S(2)}) copy-start(bf16[512,512]{1,0:T(8,128)(2,1)} %constant.8.clone.table_ref) | copy-start | bytes 1572868

commit v4 on v3

--- a/solution.py
+++ b/solution.py
@@ -46,40 +46,36 @@
     return parts.reshape(2 * F, LAGS).astype(ml_dtypes.bfloat16)
 
 
-def band_block():
-    rows = np.arange(512)[:, None] - 128
-    return (np.abs(rows - np.arange(256)[None, :]) <= HALF).astype(ml_dtypes.bfloat16)
-
-
 def normalise(record, band):
-    x = record.reshape(SUB * NW, L)
+    x = record.reshape(SUB * NW, L).T
     magnitude = jnp.abs(x)
-    quarters = []
+    runs = []
     for j in range(4):
-        low, high = max(256 * j - 128, 0), min(256 * j + 384, L)
-        first = low - (256 * j - 128)
-        sums = jnp.dot(
-            magnitude[:, low:high],
-            band[first : first + high - low, :],
-            preferred_element_type=jnp.float32,
-        )
-        places = 256 * j + lax.broadcasted_iota(jnp.int32, (1, 256), 1)
-        counts = jnp.minimum(places + HALF, L - 1) - jnp.maximum(places - HALF, 0) + 1
-        amplitude = sums * (1.0 / counts.astype(jnp.float32)) + 1e-05
-        quarters.append(x[:, 256 * j : 256 * j + 256].astype(jnp.float32) / amplitude)
-    even = [(quarters[q] + quarters[q + 2]).astype(jnp.bfloat16) for q in range(2)]
-    odd = [(quarters[q] - quarters[q + 2]).astype(jnp.bfloat16) for q in range(2)]
-    return jnp.concatenate(even, axis=1), jnp.concatenate(odd, axis=1)
+        rows = band[64 if j == 0 else 0 : 320 if j == 3 else 384, :]
+        run = jnp.dot(rows, magnitude[256 * j : 256 * j + 256], preferred_element_type=jnp.float32)
+        blocks = [run[64 * i : 64 * i + 64] for i in range(run.shape[0] // 64)]
+        runs.append([None] * (j == 0) + blocks + [None] * (j == 3))
+    edge = lax.broadcasted_iota(jnp.int32, (64, 1), 0).astype(jnp.float32)
+    pieces = []
+    for i in range(16):
+        j, place = divmod(i, 4)
+        sums = runs[j][place + 1]
+        if place == 0 and j > 0:
+            sums = sums + runs[j - 1][5]
+        if place == 3 and j < 3:
+            sums = sums + runs[j + 1][0]
+        inverse = 1.0 / (HALF + 1 + edge) if i == 0 else 1.0 / (2 * HALF - edge) if i == 15 else 1.0 / (2 * HALF + 1)
+        pieces.append(x[64 * i : 64 * i + 64].astype(jnp.float32) / (sums * inverse + 1e-05))
+    even = [(pieces[i] + pieces[i + 8]).astype(jnp.bfloat16) for i in range(8)]
+    odd = [(pieces[i] - pieces[i + 8]).astype(jnp.bfloat16) for i in range(8)]
+    return jnp.concatenate(even, axis=0), jnp.concatenate(odd, axis=0)
 
 
 def transform(table, halves):
-    return [
-        lax.dot_general(table[p], halves[p], (((1,), (1,)), ((), ())), preferred_element_type=jnp.float32)
-        for p in range(2)
-    ]
-
-
-def store_white(wide, spectra, flag, channel):
+    return [jnp.dot(table[p], halves[p], preferred_element_type=jnp.float32) for p in range(2)]
+
+
+def store_white(wide, spectra, flag, channel, out_ref):
     lanes = lax.broadcasted_iota(jnp.int32, (8, NW), 0)
     place = [8 * (v // 2) for v in range(32)]
     real = [spectra[v % 2][place[v] : place[v] + 8] for v in range(32)]
@@ -97,29 +93,37 @@
         scale = lax.rsqrt(smooth * 0.2 + floor) * flag
         for s, part in ((0, real), (1, imag)):
             wide[pl.ds((2 * v + s) * 8 * PITCH + channel, 8, stride=PITCH), :] = part[v] * scale
-
-
-def whiten_kernel(flags_hbm, record_hbm, band_hbm, table_hbm, out_ref, record, band, table, wide, flags, sems):
+            if channel == NC - 1:
+                for u in range(8):
+                    place = ((2 * v + s) * 8 + u) * PITCH
+                    row = ((16 * u + v // 2) * 4 + 2 * s + v % 2) * NC
+                    out_ref[row : row + NC, :] = wide[place : place + NC, :].astype(jnp.bfloat16)
+
+
+def whiten_kernel(flags_hbm, record_hbm, table_hbm, out_ref, record, band, table, wide, flags, sems):
     count = NC // SUB
     parts = [pl.ds(t * SUB, SUB) for t in range(count)]
     copies = [pltpu.make_async_copy(record_hbm.at[p], record.at[p], sems.at[t]) for t, p in enumerate(parts)]
     copies += [
-        pltpu.make_async_copy(band_hbm, band, sems.at[count]),
-        pltpu.make_async_copy(table_hbm, table, sems.at[count + 1]),
-        pltpu.make_async_copy(flags_hbm, flags, sems.at[count + 2]),
+        pltpu.make_async_copy(table_hbm, table, sems.at[count]),
+        pltpu.make_async_copy(flags_hbm, flags, sems.at[count + 1]),
     ]
-    for t in [0, 1, count, count + 1, count + 2, *range(2, count)]:
+    for t in [0, 1, count, count + 1, *range(2, count)]:
         copies[t].start()
+    gap = lax.broadcasted_iota(jnp.int32, (384, 256), 0) - lax.broadcasted_iota(jnp.int32, (384, 256), 1) - 64
+    band[...] = jnp.where(jnp.abs(gap) <= HALF, 1.0, 0.0).astype(jnp.bfloat16)
     halves, spectra = {}, {}
     for t in range(count + 2):
         if t < count:
             if t == 0:
-                for copy in copies[:2] + copies[count : count + 2]:
+                for copy in copies[:2]:
                     copy.wait()
             if t == 2:
-                for copy in copies[2:count] + copies[count + 2 :]:
+                for copy in copies[2:count] + copies[count + 1 :]:
                     copy.wait()
             halves[t] = normalise(record[t * SUB : (t + 1) * SUB], band)
+        if t == 1:
+            copies[count].wait()
         if 0 <= t - 1 < count:
             spectra[t - 1] = transform(table, halves.pop(t - 1))
         if 0 <= t - 2 < count:
@@ -127,32 +131,27 @@
             for c in range(SUB):
                 cut = slice(c * NW, (c + 1) * NW)
                 channel = (t - 2) * SUB + c
-                store_white(wide, (even[:, cut], odd[:, cut]), flags[channel].astype(jnp.float32), channel)
-    for f in range(F):
-        for s in range(2):
-            place = ((2 * (f % 32) + s) * 8 + f // 32) * PITCH
-            row = ((f // 2) * 4 + 2 * s + f % 2) * NC
-            out_ref[row : row + NC, :] = wide[place : place + NC, :].astype(jnp.bfloat16)
+                store_white(wide, (even[:, cut], odd[:, cut]), flags[channel].astype(jnp.float32), channel, out_ref)
 
 
 def whiten(record, flags):
     rows = 2 * F * NC
     white = pl.pallas_call(
         whiten_kernel,
-        in_specs=[pl.BlockSpec(memory_space=pltpu.HBM)] * 4,
+        in_specs=[pl.BlockSpec(memory_space=pltpu.HBM)] * 3,
         out_specs=pl.BlockSpec(memory_space=pltpu.VMEM),
         out_shape=jax.ShapeDtypeStruct((rows, NW), jnp.bfloat16),
         scratch_shapes=[
             pltpu.VMEM((NC, NW, L), jnp.bfloat16),
-            pltpu.VMEM((512, 256), jnp.bfloat16),
+            pltpu.VMEM((384, 256), jnp.bfloat16),
             pltpu.VMEM((2, F, L // 2), jnp.bfloat16),
             pltpu.VMEM((2 * F * PITCH, NW), jnp.float32),
             pltpu.SMEM((NC,), jnp.int32),
-            pltpu.SemaphoreType.DMA((NC // SUB + 3,)),
+            pltpu.SemaphoreType.DMA((NC // SUB + 2,)),
         ],
         compiler_params=pltpu.CompilerParams(vmem_limit_bytes=40 * MIB),
         cost_estimate=pl.CostEstimate(flops=2 * 2048 * 1024 * 1024, bytes_accessed=8 * MIB, transcendentals=1 << 21),
-    )(*[pltpu.with_memory_space_constraint(jnp.asarray(a), pltpu.HBM) for a in (flags, record, band_block(), dft_rows())])
+    )(*[pltpu.with_memory_space_constraint(jnp.asarray(a), pltpu.HBM) for a in (flags, record, dft_rows())])
     return white.reshape(N_DEV, 4, NC, NW)
 
 

time: 69.3 us -> 69 us (level)
  no operation moved by 1% of the time
where the time goes in v4:
time: 69 us; the launch traced here: 68.8 us
  blocking collectives  60 us (87%)
  Pallas kernels  8.84 us (13%)
    all_to_all x1, blocking collectives, per_device(): white = lax.all_to_all(whiten(record, flags), BOTH, 0, 0, tiled=True)  42 us
    all_to_all x1, blocking collectives, per_device(): spectra = lax.all_to_all(cross(white), BOTH, 0, 0, tiled=True)  18 us
    pallas_call x1, Pallas kernels, whiten(): pl.pallas_call(whiten_kernel, in_specs=[pl.BlockSpec(memory_space=pltpu.H...  6.13 us

profile of v4, /device:TPU:1, one launch (start us, length us, event | category | flops | bytes accessed | tf_op | source)
XLA Modules:
  0.0 68.8 jit_solution(3999231644815820848)
XLA Ops:
  0.0 6.1 %shard_map.46 = bf16[8192,128]{1,0:T(8,128)(2,1)S(1)} custom-call(s32[16]{0:T(128)} %flags_hbm.1, bf16[16,128,1024]{2,1,0:T(8,128)(2,1)} %record_hbm.1, bf16[2,256,512]{2,1,0:T(8,128)(2,1)} %constant.4.clone.table_hbm), custom_call_target="tpu_custom_call" | custom-call | flops 4294967296 | bytes 8388608 | tf_op jit(solution)/shard_map/pallas_call | solution.py:139
  6.1 42.0 %all_to_all.10 = bf16[128,4,16,128]{3,2,1,0:T(8,128)(2,1)S(1)} all-to-all(bf16[128,4,16,128]{3,2,1,0:T(8,128)(2,1)S(1)} %bitcast.3), channel_id=1, replica_groups=mesh['chan'=16,'tm'=8] {'chan','tm'}, dimensions={0} | all-to-all | bytes 4194304 | tf_op jit(solution)/shard_map/all_to_all | solution.py:226
  48.1 0.0 copy-start
  48.1 1.4 %shard_map.47 = bf16[16,8,16,128]{3,2,1,0:T(8,128)(2,1)S(1)} custom-call(bf16[16,8,4,16,128]{4,3,2,1,0:T(8,128)(2,1)S(1)} %bitcast.4), custom_call_target="tpu_custom_call" | custom-call | flops 1073741824 | bytes 3145728 | tf_op jit(solution)/shard_map/pallas_call | solution.py:183
  49.5 18.0 %all_to_all.11.cross_ref = bf16[128,16,128]{2,1,0:T(8,128)(2,1)S(1)} all-to-all(bf16[128,16,128]{2,1,0:T(8,128)(2,1)S(1)} %bitcast.5), channel_id=1, replica_groups=mesh['chan'=16,'tm'=8] {'chan','tm'}, dimensions={0} | all-to-all | bytes 1048576 | tf_op jit(solution)/shard_map/all_to_all | solution.py:227
  67.5 0.0 copy-done
  67.5 1.4 %shard_map.48 = f32[16,32,512]{2,1,0:T(8,128)} custom-call(bf16[128,16,128]{2,1,0:T(8,128)(2,1)S(1)} %all_to_all.11.cross_ref, bf16[512,512]{1,0:T(8,128)(2,1)S(1)} %copy-done), custom_call_target="tpu_custom_call" | custom-call | flops 268435456 | bytes 2097152 | tf_op jit(solution)/shard_map/pallas_call | solution.py:211
Async XLA Ops:
  48.1 19.4 %copy-start = (bf16[512,512]{1,0:T(8,128)(2,1)S(1)}, bf16[512,512]{1,0:T(8,128)(2,1)}, u32[]{:S(2)}) copy-start(bf16[512,512]{1,0:T(8,128)(2,1)} %constant.5.clone.table_ref) | copy-start | bytes 1572868

commit v5 on v4

--- a/solution.py
+++ b/solution.py
@@ -84,12 +84,13 @@
     before = [jnp.where(lanes == 0, 0.0, pltpu.roll(power[v], 1, 0)) for v in (30, 31)]
     after = [jnp.where(lanes == 7, 0.0, pltpu.roll(power[v], 7, 0)) for v in (0, 1)]
     padded = before + power + after
+    pairs = [padded[v] + padded[v + 1] for v in range(35)]
     total = power[0]
     for v in range(1, 32):
         total = total + power[v]
     floor = jnp.sum(total, axis=0, keepdims=True) * (0.1 / F) + 1e-06
     for v in range(32):
-        smooth = padded[v] + padded[v + 1] + padded[v + 2] + padded[v + 3] + padded[v + 4]
+        smooth = pairs[v] + pairs[v + 2] + padded[v + 4]
         scale = lax.rsqrt(smooth * 0.2 + floor) * flag
         for s, part in ((0, real), (1, imag)):
             wide[pl.ds((2 * v + s) * 8 * PITCH + channel, 8, stride=PITCH), :] = part[v] * scale
@@ -145,7 +146,7 @@
             pltpu.VMEM((NC, NW, L), jnp.bfloat16),
             pltpu.VMEM((384, 256), jnp.bfloat16),
             pltpu.VMEM((2, F, L // 2), jnp.bfloat16),
-            pltpu.VMEM((2 * F * PITCH, NW), jnp.float32),
+            pltpu.VMEM(((2 * F + 8) * PITCH, NW), jnp.float32),
             pltpu.SMEM((NC,), jnp.int32),
             pltpu.SemaphoreType.DMA((NC // SUB + 2,)),
         ],
@@ -213,7 +214,7 @@
         out_shape=jax.ShapeDtypeStruct((NC, ND, LAGS), jnp.float32),
         out_specs=pl.BlockSpec(memory_space=pltpu.HBM),
         scratch_shapes=[
-            pltpu.VMEM((N_DEV * PITCH, 4 * ND), jnp.float32),
+            pltpu.VMEM(((N_DEV + 8) * PITCH, 4 * ND), jnp.float32),
             pltpu.VMEM((NC, ND, LAGS), jnp.float32),
             pltpu.SemaphoreType.DMA((N_OUT,)),
         ],

time: 69 us -> 68.9 us (level)
  no operation moved by 1% of the time
where the time goes in v5:
time: 68.9 us; the launch traced here: 68.8 us
  blocking collectives  60 us (87%)
  Pallas kernels  8.8 us (13%)
    all_to_all x1, blocking collectives, per_device(): white = lax.all_to_all(whiten(record, flags), BOTH, 0, 0, tiled=True)  42 us
    all_to_all x1, blocking collectives, per_device(): spectra = lax.all_to_all(cross(white), BOTH, 0, 0, tiled=True)  18 us
    pallas_call x1, Pallas kernels, whiten(): pl.pallas_call(whiten_kernel, in_specs=[pl.BlockSpec(memory_space=pltpu.H...  6.09 us

profile of v5, /device:TPU:1, one launch (start us, length us, event | category | flops | bytes accessed | tf_op | source)
XLA Modules:
  0.0 68.8 jit_solution(5392386651793619357)
XLA Ops:
  0.0 6.1 %shard_map.46 = bf16[8192,128]{1,0:T(8,128)(2,1)S(1)} custom-call(s32[16]{0:T(128)} %flags_hbm.1, bf16[16,128,1024]{2,1,0:T(8,128)(2,1)} %record_hbm.1, bf16[2,256,512]{2,1,0:T(8,128)(2,1)} %constant.4.clone.table_hbm), custom_call_target="tpu_custom_call" | custom-call | flops 4294967296 | bytes 8388608 | tf_op jit(solution)/shard_map/pallas_call | solution.py:140
  6.1 42.0 %all_to_all.10 = bf16[128,4,16,128]{3,2,1,0:T(8,128)(2,1)S(1)} all-to-all(bf16[128,4,16,128]{3,2,1,0:T(8,128)(2,1)S(1)} %bitcast.3), channel_id=1, replica_groups=mesh['chan'=16,'tm'=8] {'chan','tm'}, dimensions={0} | all-to-all | bytes 4194304 | tf_op jit(solution)/shard_map/all_to_all | solution.py:227
  48.1 0.0 copy-start
  48.1 1.4 %shard_map.47 = bf16[16,8,16,128]{3,2,1,0:T(8,128)(2,1)S(1)} custom-call(bf16[16,8,4,16,128]{4,3,2,1,0:T(8,128)(2,1)S(1)} %bitcast.4), custom_call_target="tpu_custom_call" | custom-call | flops 1073741824 | bytes 3145728 | tf_op jit(solution)/shard_map/pallas_call | solution.py:184
  49.4 18.0 %all_to_all.11.cross_ref = bf16[128,16,128]{2,1,0:T(8,128)(2,1)S(1)} all-to-all(bf16[128,16,128]{2,1,0:T(8,128)(2,1)S(1)} %bitcast.5), channel_id=1, replica_groups=mesh['chan'=16,'tm'=8] {'chan','tm'}, dimensions={0} | all-to-all | bytes 1048576 | tf_op jit(solution)/shard_map/all_to_all | solution.py:228
  67.4 0.0 copy-done
  67.4 1.4 %shard_map.48 = f32[16,32,512]{2,1,0:T(8,128)} custom-call(bf16[128,16,128]{2,1,0:T(8,128)(2,1)S(1)} %all_to_all.11.cross_ref, bf16[512,512]{1,0:T(8,128)(2,1)S(1)} %copy-done), custom_call_target="tpu_custom_call" | custom-call | flops 268435456 | bytes 2097152 | tf_op jit(solution)/shard_map/pallas_call | solution.py:212
Async XLA Ops:
  48.1 19.4 %copy-start = (bf16[512,512]{1,0:T(8,128)(2,1)S(1)}, bf16[512,512]{1,0:T(8,128)(2,1)}, u32[]{:S(2)}) copy-start(bf16[512,512]{1,0:T(8,128)(2,1)} %constant.5.clone.table_ref) | copy-start | bytes 1572868

commit v6 on v5

--- a/solution.py
+++ b/solution.py
@@ -65,9 +65,9 @@
         if place == 3 and j < 3:
             sums = sums + runs[j + 1][0]
         inverse = 1.0 / (HALF + 1 + edge) if i == 0 else 1.0 / (2 * HALF - edge) if i == 15 else 1.0 / (2 * HALF + 1)
-        pieces.append(x[64 * i : 64 * i + 64].astype(jnp.float32) / (sums * inverse + 1e-05))
-    even = [(pieces[i] + pieces[i + 8]).astype(jnp.bfloat16) for i in range(8)]
-    odd = [(pieces[i] - pieces[i + 8]).astype(jnp.bfloat16) for i in range(8)]
+        pieces.append(x[64 * i : 64 * i + 64] * (1.0 / (sums * inverse + 1e-05)).astype(jnp.bfloat16))
+    even = [pieces[i] + pieces[i + 8] for i in range(8)]
+    odd = [pieces[i] - pieces[i + 8] for i in range(8)]
     return jnp.concatenate(even, axis=0), jnp.concatenate(odd, axis=0)
 
 

time: 68.9 us -> 68.7 us (level)
  no operation moved by 1% of the time
where the time goes in v6:
time: 68.7 us; the launch traced here: 68.6 us
  blocking collectives  60 us (87%)
  Pallas kernels  8.56 us (12%)
    all_to_all x1, blocking collectives, per_device(): white = lax.all_to_all(whiten(record, flags), BOTH, 0, 0, tiled=True)  42 us
    all_to_all x1, blocking collectives, per_device(): spectra = lax.all_to_all(cross(white), BOTH, 0, 0, tiled=True)  18 us
    pallas_call x1, Pallas kernels, whiten(): pl.pallas_call(whiten_kernel, in_specs=[pl.BlockSpec(memory_space=pltpu.H...  5.84 us

profile of v6, /device:TPU:1, one launch (start us, length us, event | category | flops | bytes accessed | tf_op | source)
XLA Modules:
  0.0 68.6 jit_solution(13725465887112957873)
XLA Ops:
  0.0 5.8 %shard_map.46 = bf16[8192,128]{1,0:T(8,128)(2,1)S(1)} custom-call(s32[16]{0:T(128)} %flags_hbm.1, bf16[16,128,1024]{2,1,0:T(8,128)(2,1)} %record_hbm.1, bf16[2,256,512]{2,1,0:T(8,128)(2,1)} %constant.4.clone.table_hbm), custom_call_target="tpu_custom_call" | custom-call | flops 4294967296 | bytes 8388608 | tf_op jit(solution)/shard_map/pallas_call | solution.py:140
  5.8 42.0 %all_to_all.10 = bf16[128,4,16,128]{3,2,1,0:T(8,128)(2,1)S(1)} all-to-all(bf16[128,4,16,128]{3,2,1,0:T(8,128)(2,1)S(1)} %bitcast.3), channel_id=1, replica_groups=mesh['chan'=16,'tm'=8] {'chan','tm'}, dimensions={0} | all-to-all | bytes 4194304 | tf_op jit(solution)/shard_map/all_to_all | solution.py:227
  47.8 0.0 copy-start
  47.8 1.4 %shard_map.47 = bf16[16,8,16,128]{3,2,1,0:T(8,128)(2,1)S(1)} custom-call(bf16[16,8,4,16,128]{4,3,2,1,0:T(8,128)(2,1)S(1)} %bitcast.4), custom_call_target="tpu_custom_call" | custom-call | flops 1073741824 | bytes 3145728 | tf_op jit(solution)/shard_map/pallas_call | solution.py:184
  49.2 18.0 %all_to_all.11.cross_ref = bf16[128,16,128]{2,1,0:T(8,128)(2,1)S(1)} all-to-all(bf16[128,16,128]{2,1,0:T(8,128)(2,1)S(1)} %bitcast.5), channel_id=1, replica_groups=mesh['chan'=16,'tm'=8] {'chan','tm'}, dimensions={0} | all-to-all | bytes 1048576 | tf_op jit(solution)/shard_map/all_to_all | solution.py:228
  67.2 0.0 copy-done
  67.2 1.4 %shard_map.48 = f32[16,32,512]{2,1,0:T(8,128)} custom-call(bf16[128,16,128]{2,1,0:T(8,128)(2,1)S(1)} %all_to_all.11.cross_ref, bf16[512,512]{1,0:T(8,128)(2,1)S(1)} %copy-done), custom_call_target="tpu_custom_call" | custom-call | flops 268435456 | bytes 2097152 | tf_op jit(solution)/shard_map/pallas_call | solution.py:212
Async XLA Ops:
  47.8 19.4 %copy-start = (bf16[512,512]{1,0:T(8,128)(2,1)S(1)}, bf16[512,512]{1,0:T(8,128)(2,1)}, u32[]{:S(2)}) copy-start(bf16[512,512]{1,0:T(8,128)(2,1)} %constant.5.clone.table_ref) | copy-start | bytes 1572868
